TPU v7x, 256 devices: a whole 4x4x8 slice. The times are simulated.
256 devices in a mesh: row: 4 (over y), col: 64 (over x, z, core).
Axes of the slice: x: 4, y: 4, z: 8, core: 2. Of those that a mesh axis runs over, the one named last changes fastest.
Arguments:
- features_x: float32 [16384, 256], P('row'), may hold values from -6 to 6
- scale_x: float32 [16384], P('row'), may hold values from 0.3 to 9
- adjoint_x: float32 [16384], P('row'), may hold values from -6 to 6
- features_y: float32 [65536, 256], P('col'), may hold values from -6 to 6
- scale_y: float32 [65536], P('col'), may hold values from 0.3 to 9
- adjoint_y: float32 [65536], P('col'), may hold values from -6 to 6
Outputs:
- grad_x: float32 [16384, 256], P(('row', 'col'))
- grad_y: float32 [65536, 256], P('col', 'row')
All inputs are finite; a program needn't handle non-finite values.
Results may differ from a plain program's by a relative error of at most 0.0003.
The roundings to bfloat16 on the way count: a program that leaves them out, or rounds other values in their place, can miss the bound.
Values sent between devices are 32-bit elements; how exact they have to be, the bound alone decides.
A program may use at most 64 MiB of HBM per device.

v0:
```python
import math

import jax
import jax.numpy as jnp
from jax import lax
from jax.sharding import PartitionSpec as P

SWEEPS = 2


kernel_gain = 0.5


def plan_rows(rows_x, rows_u, cols_y, scale_y, factor):
    scores = lax.dot_general(
        rows_x, cols_y, (((1,), (1,)), ((), ())), preferred_element_type=jnp.float32
    )
    return rows_u[:, None] * jnp.exp(scores * factor) * scale_y[None, :]


def finish_rows(partial_value, base, totals):
    return base - lax.psum(partial_value, "col") / totals


def body(features_x, scale_x, adjoint_x, features_y, scale_y, adjoint_y):
    width = features_x.shape[1]
    factor = kernel_gain / math.sqrt(width)
    xbf = features_x.astype(jnp.bfloat16)
    ybf = features_y.astype(jnp.bfloat16)
    nrows = xbf.shape[0]
    ncols = ybf.shape[0]
    whole = plan_rows(xbf, scale_x, ybf, scale_y, factor)

    def fetch():
        return whole

    nblocks = nrows // nrows
    starts = jnp.arange(nblocks, dtype=jnp.int32) * nrows

    def over_blocks(step_fn, init):
        return lax.scan(step_fn, init, starts)

    def first(acc, start):
        plan = fetch()
        return (acc + jnp.sum(plan, axis=0), jnp.sum(plan, axis=1))

    col_part, row_part = over_blocks(first, jnp.zeros((ncols,), jnp.float32))
    row_tot = lax.psum(row_part.reshape(nrows), "col")
    col_tot = lax.psum(col_part, "row")
    adj_row = adjoint_x
    adj_col = adjoint_y
    for turn_index in range(SWEEPS):
        current = adj_col

        def mix_fn(acc, start):
            return (acc, jnp.dot(fetch(), current, precision=lax.Precision.HIGHEST))

        unused, mixed = over_blocks(mix_fn, jnp.zeros((), jnp.float32))
        adj_row = finish_rows(mixed.reshape(nrows), adjoint_x, row_tot)
        fresh_row = adj_row

        def back_fn(acc, start):
            return (
                acc + jnp.dot(fresh_row, fetch(), precision=lax.Precision.HIGHEST),
                jnp.zeros((), jnp.float32),
            )

        col_part, unused_two = over_blocks(back_fn, jnp.zeros((ncols,), jnp.float32))
        adj_col = adjoint_y - lax.psum(col_part, "row") / col_tot
    final_row = adj_row
    final_col = adj_col

    def col_fn(acc, start):
        weight_block = (fetch() * (final_row[:, None] + final_col[None, :])).astype(jnp.bfloat16)
        term = lax.dot_general(
            weight_block, xbf, (((0,), (0,)), ((), ())), preferred_element_type=jnp.float32
        )
        rows_grad = factor * jnp.dot(weight_block, ybf, preferred_element_type=jnp.float32)
        return (acc + term, rows_grad)

    acc_y, row_pieces = over_blocks(col_fn, jnp.zeros((ncols, width), jnp.float32))
    row_stack = row_pieces.reshape(nrows, width)
    grad_y = lax.psum_scatter(factor * acc_y, "row", scatter_dimension=1, tiled=True)
    grad_x = lax.psum_scatter(row_stack, "col", scatter_dimension=0, tiled=True)
    return (grad_x, grad_y)


def solution(mesh):
    in_specs = (P("row", None), P("row"), P("row"), P("col", None), P("col"), P("col"))
    out_specs = (P(("row", "col"), None), P("col", "row"))
    return jax.shard_map(body, mesh=mesh, in_specs=in_specs, out_specs=out_specs, check_vma=False)
```

profile of v0, /device:TPU:32, one launch (start us, length us, event | category | flops | bytes accessed | tf_op | source)
XLA Modules:
  0.0 780.9 jit_solution(17649815705767460479)
XLA Ops:
  7.2 0.0 reduce-scatter.5.cloned.1.call-start
  7.2 6.9 fusion.4
  14.1 0.0 copy-start.2
  14.1 5.7 copy-done
  19.8 14.3 %fusion.5 = f32[1,4096]{1,0:T(1,128)S(1)} fusion(f32[4096,1024]{1,0:T(8,128)S(1)} %get-tuple-element.72, f32[1024,1]{0,1:T(1,128)S(1)} %bitcast.22), kind=kOutput, calls=%fused_computation.13 | convolution fusion | flops 50331648 | bytes 16797696 | tf_op jit(solution)/shard_map/while/body/eval_jaxpr/dot_general | solution.py:56
  34.1 248.3 %all-reduce = (f32[4096]{0:T(1024)S(1)}, f32[4096]{0:T(1024)S(1)}) all-reduce(f32[4096]{0:T(1024)S(1)} %bitcast.19, f32[4096]{0:T(1024)S(1)} %get-tuple-element.59), channel_id=1, replica_groups=mesh['row'=4,'col'=64] {'col'}, use_global_device_ids=true, to_apply=%region_0.1 | all-reduce | flops 8192 | bytes 65536 | tf_op jit(solution)/shard_map/psum | solution.py:22
  282.4 0.0 copy-done.2
  282.4 11.5 %fusion.6 = f32[1,1024]{1,0:T(1,128)S(1)} fusion(f32[4096,1]{0,1:T(1,128)S(1)} %bitcast.21, f32[4096,1024]{1,0:T(8,128)} %copy-done), kind=kOutput, calls=%fused_computation.14 | convolution fusion | flops 50331648 | bytes 16797696 | tf_op jit(solution)/shard_map/while/body/eval_jaxpr/dot_general | solution.py:64
  293.9 10.8 %all-reduce.1 = (f32[1024]{0:T(1024)S(1)}, f32[1024]{0:T(1024)S(1)}) all-reduce(f32[1024]{0:T(1024)S(1)} %bitcast.24, f32[1024]{0:T(1024)S(1)} %get-tuple-element.58), channel_id=1, replica_groups=mesh['row'=4,'col'=64] {'row'}, use_global_device_ids=true, to_apply=%region_3.4 | all-reduce | flops 2048 | bytes 16384 | tf_op jit(solution)/shard_map/psum | solution.py:69
  304.8 17.5 %fusion.7 = f32[1,4096]{1,0:T(1,128)S(1)} fusion(f32[4096,1024]{1,0:T(8,128)} %copy-done, f32[1024,1]{0,1:T(1,128)S(1)} %bitcast.23), kind=kOutput, calls=%fused_computation.15 | convolution fusion | flops 50331648 | bytes 16797696 | tf_op jit(solution)/shard_map/while/body/eval_jaxpr/dot_general | solution.py:56
  322.3 246.4 %psum.46 = f32[4096]{0:T(1024)S(1)} all-reduce(f32[4096]{0:T(1024)S(1)} %bitcast.20), channel_id=1, replica_groups=mesh['row'=4,'col'=64] {'col'}, use_global_device_ids=true, to_apply=%region_6.7 | all-reduce | flops 4096 | bytes 32768 | tf_op jit(solution)/shard_map/psum | solution.py:22
  568.7 11.5 %fusion.8 = f32[1,1024]{1,0:T(1,128)S(1)} fusion(f32[4096,1]{0,1:T(1,128)S(1)} %bitcast.18, f32[4096,1024]{1,0:T(8,128)} %copy-done), kind=kOutput, calls=%fused_computation.16 | convolution fusion | flops 50331648 | bytes 16797696 | tf_op jit(solution)/shard_map/while/body/eval_jaxpr/dot_general | solution.py:64
  580.1 7.7 psum.47
  587.9 0.0 copy-start.5
  587.9 7.5 multiply_convert_fusion
  595.4 3.2 copy-done.1
  598.6 0.0 copy-done.4
  598.6 3.4 convolution_multiply_fusion.1
  602.1 0.0 reduce-scatter.5.cloned.1.call-update
  602.1 0.0 reduce-scatter.3.cloned.1.call-start
  602.1 7.7 convolution_multiply_fusion
  609.9 0.0 reduce-scatter.3.cloned.1.call-update
  609.9 16.3 %reduce-scatter.5.cloned.1.call-done = f32[1024,64]{0,1:T(8,128)} async-done(((f32[1024,256]{0,1:T(8,128)}), f32[1024,64]{0,1:T(8,128)}) %reduce-scatter.5.cloned.1.call-update) | async-done | bytes 262160 | tf_op jit(solution)/shard_map/reduce_scatter | solution.py:83
  626.2 147.8 %reduce-scatter.3.cloned.1.call-done = f32[64,256]{1,0:T(8,128)} async-done(((f32[4096,256]{1,0:T(8,128)}), f32[64,256]{1,0:T(8,128)}) %reduce-scatter.3.cloned.1.call-update) | async-done | bytes 65552 | tf_op jit(solution)/shard_map/reduce_scatter | solution.py:84
  (10 shorter events, 0.0 us)
Async XLA Ops:
  7.2 12.7 %copy-start.3 = (f32[1024]{0:T(1024)S(1)}, f32[1024]{0:T(1024)}, u32[]{:S(2)}) copy-start(f32[1024]{0:T(1024)} %param.11) | copy-start | bytes 12292
  7.2 619.0 %reduce-scatter.5.cloned.1.call-start = ((), (), s32[]{:S(2)}) async-start(), calls=%async_computation.3 | async-start | bytes 1310720 | tf_op jit(solution)/shard_map/reduce_scatter | solution.py:83
  14.1 5.7 copy-start
  14.1 268.3 %copy-start.2 = (f32[4096]{0:T(1024)S(1)}, f32[4096]{0:T(1024)}, u32[]{:S(2)}) copy-start(f32[4096]{0:T(1024)} %param.8) | copy-start | bytes 49156
  587.9 10.8 %copy-start.4 = (f32[4096,256]{1,0:T(8,128)S(1)}, f32[4096,256]{1,0:T(8,128)}, u32[]{:S(2)}) copy-start(f32[4096,256]{1,0:T(8,128)} %param.6) | copy-start | bytes 12582916
  587.9 14.3 %copy-start.5 = (f32[1024,256]{1,0:T(8,128)S(1)}, f32[1024,256]{1,0:T(8,128)}, u32[]{:S(2)}) copy-start(f32[1024,256]{1,0:T(8,128)} %param.9) | copy-start | bytes 3145732
  595.4 3.2 copy-start.1
  602.1 172.0 %reduce-scatter.3.cloned.1.call-start = ((), (), s32[]{:S(2)}) async-start(), calls=%async_computation.2 | async-start | bytes 4259840 | tf_op jit(solution)/shard_map/reduce_scatter | solution.py:84
Sparse Core Ops, SparseCore 0:
  602.2 23.9 reduce-scatter.4
  631.4 142.5 reduce-scatter.2
where the time goes:
time: 782 us; the launch traced here: 781 us
  blocking collectives  513 us (66%)
  waiting for transfers between devices  164 us (21%)
  matrix products  72.8 us (9%)
  between operations  14.1 us (2%)
  local copies, waits for them, and re-layouts  8.93 us (1%)
    psum x2, blocking collectives, finish_rows(): return base - lax.psum(partial_value, 'col') / totals  495 us
    reduce_scatter x1, waiting for transfers between devices, body(): grad_x = lax.psum_scatter(row_stack, 'col', scatter_dimension=0, tiled=True)  148 us
    dot_general x2, matrix products, mix_fn(): return (acc, jnp.dot(fetch(), current, precision=lax.Precision.HIGHEST))  31.8 us
    dot_general x2, matrix products, back_fn(): jnp.dot(fresh_row, fetch(), precision=lax.Precision.HIGHEST)  22.9 us
    psum x2, blocking collectives, body(): adj_col = adjoint_y - lax.psum(col_part, 'row') / col_tot  18.6 us
    reduce_scatter x1, waiting for transfers between devices, body(): lax.psum_scatter(factor * acc_y, 'row', scatter_dimension=1, tiled=True)  16.3 us
  transfers between devices with their start and end apart: 2, of which 2 were waited for; matrix products, arithmetic and copies ran while one was open for 1% of the time, Pallas kernels for 0%

commit v1 on v0

v1 whole, which is shorter than its diff:
```python
import functools
import math

import jax
import jax.numpy as jnp
from jax import lax
from jax.experimental import pallas as pl
from jax.experimental.pallas import tpu as pltpu
from jax.sharding import PartitionSpec as P

KERNEL_GAIN = 0.5
WIDTH = 256
FACTOR = KERNEL_GAIN / math.sqrt(WIDTH)
L = 128
F32 = jnp.float32
BF16 = jnp.bfloat16
MESH = pl.DeviceIdType.MESH
NX, NY, NZ = 4, 4, 8
STRIP = 256
OTHERS_Z = (4, 3, 5, 2, 6, 1, 7)
OTHERS_4 = (2, 1, 3)
GROUP_YC = tuple((a, c) for a in (2, 1, 3, 0) for c in (0, 1) if (a, c) != (0, 0))


def kernel(
    sx_ref, ax_ref, sy_ref, ay_ref, x_hbm, y_hbm, gx_ref, gy_ref,
    xf, yf, xb, yb, xt, plan, wts, syv, ayv, rowb, ub, rt, mx, axd,
    vrow, xrow, zrow, vcol, crow, avec, ctot,
    ga, gb, a1, a2, az, bp, bm, bx, gy, gyc, y1, y2,
    in_sem, sem_s, sem_r,
):
    row = lax.axis_index("row")
    col = lax.axis_index("col")
    x = col // (NZ * 2)
    z = (col // 2) % NZ
    core = col % 2
    other = 1 - core

    def at(dy=0, dx=0, dz=0, dc=0):
        return (
            lax.rem(row + dy, NY),
            (lax.rem(x + dx, NX) * NZ + lax.rem(z + dz, NZ)) * 2 + lax.rem(core + dc, 2),
        )

    count = [0]
    sent = []

    def send(src, dst, device):
        n = count[0]
        count[0] += 1
        copy = pltpu.make_async_remote_copy(
            src_ref=src, dst_ref=dst, send_sem=sem_s.at[n], recv_sem=sem_r.at[n],
            device_id=device, device_id_type=MESH,
        )
        copy.start()
        sent.append(copy)
        return copy

    loads = [
        pltpu.make_async_copy(y_hbm, yf.at[core], in_sem.at[0]),
        pltpu.make_async_copy(x_hbm.at[0, :, core], xf.at[:, 0], in_sem.at[1]),
        pltpu.make_async_copy(x_hbm.at[1, :, core], xf.at[:, 1], in_sem.at[2]),
    ]
    for copy in loads:
        copy.start()

    barrier = pltpu.get_barrier_semaphore()
    peers = (
        [at(dz=d) for d in OTHERS_Z] + [at(dx=d) for d in OTHERS_4]
        + [at(dy=a, dc=c) for a, c in GROUP_YC]
    )
    for peer in peers:
        pl.semaphore_signal(barrier, inc=1, device_id=peer, device_id_type=MESH)

    lane = lax.broadcasted_iota(jnp.int32, (16, L), 1)
    first = core == 0

    def mine(ref):
        low, high = ref[0:16, :], ref[16:32, :]
        low_r, high_r = pltpu.roll(low, 64, 1), pltpu.roll(high, 64, 1)
        return jnp.where(lane < 64, jnp.where(first, low, low_r), jnp.where(first, high_r, high))

    def spread(vec, dst):
        for m in range(16):
            dst[m * L:(m + 1) * L, :] = jnp.broadcast_to(vec[m:m + 1, :], (L, L)).T

    def gather_rows(src, dst, which):
        for m in range(16):
            dst[which, m:m + 1, :] = jnp.sum(src[m * L:(m + 1) * L, :].T, axis=0, keepdims=True)

    axd[...] = mine(ax_ref)
    spread(mine(sx_ref), ub)
    syv[core] = sy_ref[...]
    ayv[core] = ay_ref[...]
    rt[...] = jnp.zeros_like(rt)
    mx[...] = jnp.zeros_like(mx)
    for copy in loads:
        copy.wait()

    def cast_x(i, _):
        xb[pl.ds(i * L, 64), :] = xf[i, 0].astype(BF16)
        xb[pl.ds(i * L + 64, 64), :] = xf[i, 1].astype(BF16)
        return 0
    lax.fori_loop(0, 16, cast_x, 0)

    def cast_y(half):
        def step(i, _):
            yb[half, pl.ds(i * L, L), :] = yf[half, pl.ds(i * L, L), :].astype(BF16)
            return 0
        lax.fori_loop(0, 8, step, 0)
    cast_y(core)

    def fold8(v):
        return jnp.sum(v.reshape(-1, 8, L), axis=0)

    def make_plan(half):
        def strip(i, cols):
            rows = pl.ds(pl.multiple_of(i * STRIP, STRIP), STRIP)
            out = []
            for j in range(2):
                s = lax.dot_general(
                    xb[rows, :], yb[half, j * 512:(j + 1) * 512, :],
                    (((1,), (1,)), ((), ())), preferred_element_type=F32,
                )
                u = ub[rows, :]
                acc_r = rt[rows, :]
                acc_m = mx[rows, :]
                for l in range(4):
                    t = j * 4 + l
                    p = (u * jnp.exp(s[:, l * L:(l + 1) * L] * FACTOR)) * syv[half, t:t + 1, :]
                    plan[half, rows, t * L:(t + 1) * L] = p
                    acc_r += p
                    acc_m += p * ayv[half, t:t + 1, :]
                    out.append(cols[t] + fold8(p))
                rt[rows, :] = acc_r
                mx[rows, :] = acc_m
            return tuple(out)
        cols = lax.fori_loop(0, 8, strip, tuple(jnp.zeros((8, L), F32) for _ in range(8)))
        for t in range(8):
            vcol[0, pl.ds(half * 8 + t, 1), :] = jnp.sum(cols[t], axis=0, keepdims=True)

    pl.semaphore_wait(barrier, len(peers))
    sib = at(dc=1)
    fetch = [
        send(y_hbm, yf.at[core], sib),
        send(sy_ref, syv.at[core], sib),
        send(ay_ref, ayv.at[core], sib),
    ]
    make_plan(core)
    for copy in fetch:
        copy.wait_recv()
    cast_y(other)
    make_plan(other)

    def reduce_rows(n):
        copies = [
            send(vrow.at[0:n], xrow.at[n - 1, k, 0:n], at(dx=d)) for k, d in enumerate(OTHERS_4)
        ]
        return copies

    def reduce_rows_z(n, copies):
        for copy in copies:
            copy.wait_recv()
        total = vrow[0:n]
        for k in range(3):
            total = total + xrow[n - 1, k, 0:n]
        vrow[2:2 + n] = total
        return [
            send(vrow.at[2:2 + n], zrow.at[n - 1, k, 0:n], at(dz=d)) for k, d in enumerate(OTHERS_Z)
        ]

    def finish_rows(n, copies):
        for copy in copies:
            copy.wait_recv()
        total = vrow[2:2 + n]
        for k in range(7):
            total = total + zrow[n - 1, k, 0:n]
        return total

    def drain():
        for copy in sent:
            copy.wait_send()
        sent.clear()

    def reduce_cols(n):
        src = vcol.at[2 - n:2]
        copies = [
            send(src, crow.at[n - 1, k, 0:n], at(dy=a, dc=c)) for k, (a, c) in enumerate(GROUP_YC)
        ]
        for copy in copies:
            copy.wait_recv()
        total = vcol[2 - n:2]
        for k in range(7):
            total = total + crow[n - 1, k, 0:n]
        return total

    gather_rows(rt, vrow, 0)
    gather_rows(mx, vrow, 1)
    copies = reduce_rows(2)

    def turn_x(i, _):
        rows = pl.ds(pl.multiple_of(i * L, L), L)
        xt[:, rows] = xb[rows, :].T
        return 0
    lax.fori_loop(0, 16, turn_x, 0)
    copies = reduce_rows_z(2, copies)
    total = finish_rows(2, copies)
    row_tot = total[0]
    adj_row = axd[...] - total[1] / row_tot
    spread(adj_row, rowb)

    def back():
        for half in range(2):
            def strip(i, cols):
                rows = pl.ds(pl.multiple_of(i * STRIP, STRIP), STRIP)
                r = rowb[rows, :]
                return tuple(
                    cols[t] + fold8(plan[half, rows, t * L:(t + 1) * L] * r) for t in range(8)
                )
            cols = lax.fori_loop(0, 8, strip, tuple(jnp.zeros((8, L), F32) for _ in range(8)))
            for t in range(8):
                vcol[1, half * 8 + t:half * 8 + t + 1, :] = jnp.sum(cols[t], axis=0, keepdims=True)

    back()
    total = reduce_cols(2)
    ay_all = ayv[...].reshape(16, L)
    col_tot = total[0]
    ctot[...] = col_tot
    avec[...] = ay_all - total[1] / col_tot
    drain()

    def mix(i, _):
        rows = pl.ds(pl.multiple_of(i * STRIP, STRIP), STRIP)
        acc = jnp.zeros((STRIP, L), F32)
        for half in range(2):
            for t in range(8):
                acc += plan[half, rows, t * L:(t + 1) * L] * avec[half * 8 + t:half * 8 + t + 1, :]
        mx[rows, :] = acc
        return 0
    lax.fori_loop(0, 8, mix, 0)
    gather_rows(mx, vrow, 0)
    copies = reduce_rows(1)
    copies = reduce_rows_z(1, copies)
    total = finish_rows(1, copies)
    adj_row = axd[...] - total[0] / row_tot
    spread(adj_row, rowb)
    back()
    total = reduce_cols(1)
    avec[...] = ay_all - total[0] / ctot[...]
    drain()

    def weigh(i, _):
        rows = pl.ds(pl.multiple_of(i * STRIP, STRIP), STRIP)
        r = rowb[rows, :]
        for half in range(2):
            for t in range(8):
                a = avec[half * 8 + t:half * 8 + t + 1, :]
                w = plan[half, rows, t * L:(t + 1) * L] * (r + a)
                wts[half, rows, t * L:(t + 1) * L] = w.astype(BF16)
        g = jnp.dot(wts[0, rows, :], yb[0], preferred_element_type=F32)
        g += jnp.dot(wts[1, rows, :], yb[1], preferred_element_type=F32)
        g = g * FACTOR
        xq = i // 4
        for mm in range(2):
            zq = lax.rem(2 * i + mm, 8)
            for h in range(2):
                piece = g[mm * L + h * 64:mm * L + h * 64 + 64, :]
                ga[2 * h + xq, zq] = piece[:, 0:L]
                gb[zq, 2 * h + xq] = piece[:, L:2 * L]
        return 0
    lax.fori_loop(0, 8, weigh, 0)

    def mod(v, n):
        return lax.rem(v, n)

    def ring_start(g, r1, r2, fwd, bwd, me):
        far, right, left = mod(me + 2, 4), mod(me + 1, 4), mod(me + 3, 4)
        one = [send(g.at[far, 0], r1.at[0], fwd), send(g.at[far, 1], r1.at[1], bwd)]
        two = [send(g.at[right, 1], r2.at[0, 1], fwd), send(g.at[left, 0], r2.at[1, 0], bwd)]
        return one, two

    def ring_middle(g, r1, r2, fwd, bwd, me, one, two):
        right, left = mod(me + 1, 4), mod(me + 3, 4)
        one[0].wait_recv()
        g[right, 0] = g[right, 0] + r1[0]
        two.append(send(g.at[right, 0], r2.at[0, 0], fwd))
        one[1].wait_recv()
        g[left, 1] = g[left, 1] + r1[1]
        two.append(send(g.at[left, 1], r2.at[1, 1], bwd))

    def ring_end(g, r2, me, two):
        for copy in two:
            copy.wait_recv()
        g[me] = g[me] + r2[0] + r2[1]

    ga_h = ga.reshape(4, 2, 4, 64, L)
    right_x, left_x = at(dx=1), at(dx=3)
    one_a, two_a = ring_start(ga_h, a1, a2, right_x, left_x, x)

    right_z, left_z = at(dz=1), at(dz=7)
    far = mod(z + 4, 8)
    fwd = [send(gb.at[far, 0:2], bp.at[0, 0:2], right_z)]
    bwd = [send(gb.at[far, 2:4], bm.at[0, 2:4], left_z)]

    def cols_of(half, dst):
        def step(n, _):
            cols = pl.ds(pl.multiple_of(n * 256, 256), 256)
            g = jnp.dot(xt[...], wts[half, :, cols], preferred_element_type=F32) * FACTOR
            for q in range(4):
                for h in range(2):
                    dst[q, h, :, cols] = g[q * 64 + h * 32:q * 64 + h * 32 + 32, :]
            return 0
        lax.fori_loop(0, 4, step, 0)

    cols_of(other, gyc.at[0])
    swap = send(gyc.at[0], gyc.at[1], sib)

    def z_step(s):
        ahead, behind = mod(z + 4 - s, 8), mod(z + 4 + s, 8)
        fwd[-1].wait_recv()
        if s == 1:
            gb[ahead, 0:2] = gb[ahead, 0:2] + bp[0, 0:2]
        else:
            gb[ahead] = gb[ahead] + bp[s - 1]
        fwd.append(send(gb.at[ahead], bp.at[s], right_z))
        bwd[-1].wait_recv()
        if s == 1:
            gb[behind, 2:4] = gb[behind, 2:4] + bm[0, 2:4]
        else:
            gb[behind] = gb[behind] + bm[s - 1]
        bwd.append(send(gb.at[behind], bm.at[s], left_z))

    z_step(1)
    cols_of(core, gy)
    ring_middle(ga_h, a1, a2, right_x, left_x, x, one_a, two_a)
    swap.wait_recv()
    gy[...] = gy[...] + gyc[1]
    right_y, left_y = at(dy=1), at(dy=3)
    one_y, two_y = ring_start(gy, y1, y2, right_y, left_y, row)
    z_step(2)
    ring_middle(gy, y1, y2, right_y, left_y, row, one_y, two_y)
    z_step(3)
    ring_end(ga_h, a2, x, two_a)
    last_a = [send(ga.at[x, mod(z + d, 8)], az.at[k], at(dz=d)) for k, d in enumerate(OTHERS_Z)]
    fwd[-1].wait_recv()
    bwd[-1].wait_recv()
    gb[z] = gb[z] + bp[3] + bm[3]
    last_b = [send(gb.at[z, mod(x + d, 4)], bx.at[k], at(dx=d)) for k, d in enumerate(OTHERS_4)]
    ring_end(gy, y2, row, two_y)
    gy_ref[0:32, :] = gy[row, 0]
    gy_ref[32:64, :] = gy[row, 1]
    total = gb[z, x]
    for k in range(3):
        last_b[k].wait_recv()
        total = total + bx[k]
    gx_ref[:, L:2 * L] = total
    total = ga[x, z]
    for k in range(7):
        last_a[k].wait_recv()
        total = total + az[k]
    gx_ref[:, 0:L] = total
    drain()


def body(features_x, scale_x, adjoint_x, features_y, scale_y, adjoint_y):
    vmem = pl.BlockSpec(memory_space=pltpu.VMEM)
    anym = pl.BlockSpec(memory_space=pl.ANY)
    V = pltpu.VMEM
    ncopies = 96
    gx, gy = pl.pallas_call(
        kernel,
        out_shape=(
            jax.ShapeDtypeStruct((64, WIDTH), F32),
            jax.ShapeDtypeStruct((64, 1024), F32),
        ),
        in_specs=[vmem, vmem, vmem, vmem, anym, anym],
        out_specs=(vmem, vmem),
        scratch_shapes=[
            V((16, 2, 64, WIDTH), F32), V((2, 1024, WIDTH), F32),
            V((2048, WIDTH), BF16), V((2, 1024, WIDTH), BF16), V((WIDTH, 2048), BF16),
            V((2, 2048, 1024), F32), V((2, 2048, 1024), BF16),
            V((2, 8, L), F32), V((2, 8, L), F32),
            V((2048, L), F32), V((2048, L), F32), V((2048, L), F32), V((2048, L), F32), V((16, L), F32),
            V((4, 16, L), F32), V((2, 3, 2, 16, L), F32), V((2, 7, 2, 16, L), F32),
            V((2, 16, L), F32), V((2, 7, 2, 16, L), F32), V((16, L), F32), V((16, L), F32),
            V((4, 8, 64, L), F32), V((8, 4, 64, L), F32),
            V((2, 4, 64, L), F32), V((2, 2, 4, 64, L), F32), V((7, 64, L), F32),
            V((4, 4, 64, L), F32), V((4, 4, 64, L), F32), V((3, 64, L), F32),
            V((4, 2, 32, 1024), F32), V((2, 4, 2, 32, 1024), F32),
            V((2, 32, 1024), F32), V((2, 2, 32, 1024), F32),
            pltpu.SemaphoreType.DMA((3,)),
            pltpu.SemaphoreType.DMA((ncopies,)), pltpu.SemaphoreType.DMA((ncopies,)),
        ],
        compiler_params=pltpu.CompilerParams(
            collective_id=0, has_side_effects=True, vmem_limit_bytes=60 * 2**20
        ),
        cost_estimate=pl.CostEstimate(
            flops=6 * 2048 * 2048 * 256, bytes_accessed=5 * 2**20, transcendentals=2048 * 2048
        ),
        name="sinkhorn_adjoint",
    )(
        scale_x.reshape(32, L), adjoint_x.reshape(32, L),
        scale_y.reshape(8, L), adjoint_y.reshape(8, L),
        features_x.reshape(2, 16, 2, 64, WIDTH), features_y,
    )
    return gx, gy.T


def solution(mesh):
    in_specs = (P("row", None), P("row"), P("row"), P("col", None), P("col"), P("col"))
    out_specs = (P(("row", "col"), None), P("col", "row"))
    return jax.shard_map(body, mesh=mesh, in_specs=in_specs, out_specs=out_specs, check_vma=False)
```

time: 782 us -> 80.5 us (0.10)
  blocking collectives: 513 us -> 0 us
  waiting for transfers between devices: 164 us -> 0 us
  Pallas kernels: 0 us -> 76.5 us
  matrix products: 72.8 us -> 0 us
  between operations: 14.1 us -> 0.64 us
    psum x4 -> x0, blocking collectives: 513 us -> none  [the longest x2 495 us: finish_rows(): return base - lax.psum(partial_value, 'col') / totals]
    reduce_scatter x2 -> x0, waiting for transfers between devices: 164 us -> none  [the longest x1 148 us: body(): grad_x = lax.psum_scatter(row_stack, 'col', scatter_dimension=0, tiled=True)]
    pallas_call x0 -> x1, Pallas kernels: none -> 76.5 us  [body(): pl.pallas_call(kernel, out_shape=(jax.ShapeDtypeStruct((64, WIDTH), F32),...]
    dot_general x7 -> x0, matrix products: 72.8 us -> none  [the longest x2 31.8 us: mix_fn(): return (acc, jnp.dot(fetch(), current, precision=lax.Precision.HIGHEST))]
  transfers between devices with their start and end apart: 2 -> 0, of which waited for: 2 -> 0; matrix products, arithmetic and copies ran while one was open for 1% -> 0% of each run, Pallas kernels for 0% -> 0%
where the time goes in v1:
time: 80.5 us; the launch traced here: 80.3 us
  Pallas kernels  76.5 us (95%)
  local copies, waits for them, and re-layouts  3.14 us (4%)
    pallas_call x1, Pallas kernels, body(): pl.pallas_call(kernel, out_shape=(jax.ShapeDtypeStruct((64, WIDTH), F32),...  76.5 us
    unnamed x2, local copies, waits for them, and re-layouts  3.14 us

profile of v1, /device:TPU:32, one launch (start us, length us, event | category | flops | bytes accessed | tf_op | source)
XLA Modules:
  0.0 80.3 jit_solution(4613841587838926620)
XLA Ops:
  0.6 76.5 %sinkhorn_adjoint.1 = (f32[64,256]{1,0:T(8,128)}, f32[64,1024]{1,0:T(8,128)}) custom-call(f32[32,128]{1,0:T(8,128)} %bitcast.8, f32[32,128]{1,0:T(8,128)} %bitcast.9, f32[8,128]{1,0:T(8,128)} %bitcast.10, f32[8,128]{1,0:T(8,128)} %bitcast.11, f32[2,16,2,64,256]{4,3,2,1,0:T(8,128)} %bitcast.7, f32[1024,256]{1,0:T(8,128)} %y_hbm.1), custom_call_target="tpu_custom_call" | custom-call | flops 6442450944 | bytes 5242880 | tf_op jit(solution)/shard_map/sinkhorn_adjoint/pallas_call | solution.py:370
  77.1 1.5 %copy.10 = f32[64,256]{1,0:T(8,128)} copy(f32[64,256]{1,0:T(8,128)} %get-tuple-element.8) | data formatting | bytes 131072
  78.6 1.7 %copy.11 = f32[1024,64]{0,1:T(8,128)} copy(f32[1024,64]{0,1:T(8,128)} %bitcast.6) | data formatting | bytes 524288

commit v2 on v0

v2 whole, which is shorter than its diff:
```python
import functools
import math

import jax
import jax.numpy as jnp
from jax import lax
from jax.experimental import pallas as pl
from jax.experimental.pallas import tpu as pltpu
from jax.sharding import PartitionSpec as P

KERNEL_GAIN = 0.5
WIDTH = 256
FACTOR = KERNEL_GAIN / math.sqrt(WIDTH)
L = 128
F32 = jnp.float32
BF16 = jnp.bfloat16
MESH = pl.DeviceIdType.MESH
NX, NY, NZ = 4, 4, 8
STRIP = 256
HALF = 1024
RA = 40
RB = 64 - RA
OTHERS_Z = (4, 3, 5, 2, 6, 1, 7)
OTHERS_4 = (2, 1, 3)
FAR_Z = (2, 1, 3, 0)
NEAR_Z = (4, 5, 7)
GROUP_YC = tuple((a, c) for a in (2, 1, 3, 0) for c in (0, 1) if (a, c) != (0, 0))


def kernel(
    sx_ref, ax_ref, sy_ref, ay_ref, x_hbm, y_hbm, gx_ref, gy_ref,
    xf, yf, xb, yb, xt, plan, wts, syv, ayv, rowb, ub, rt, mx, axd, colacc,
    vrow, xrow, zsrc, zrow, vcol, crow, vcol2, crow2, avec, rtot, ctot,
    ga, gb, a1, a2, az, b1, bp, bm, bx, gy, gyo, gyc, y1, y2,
    in_sem, sem_s, sem_r,
):
    row = lax.axis_index("row")
    col = lax.axis_index("col")
    x = col // (NZ * 2)
    z = (col // 2) % NZ
    core = col % 2
    other = 1 - core

    def at(dy=0, dx=0, dz=0, dc=0):
        return (
            lax.rem(row + dy, NY),
            (lax.rem(x + dx, NX) * NZ + lax.rem(z + dz, NZ)) * 2 + lax.rem(core + dc, 2),
        )

    count = [0]
    sent = []

    def send(src, dst, device):
        n = count[0]
        count[0] += 1
        copy = pltpu.make_async_remote_copy(
            src_ref=src, dst_ref=dst, send_sem=sem_s.at[n], recv_sem=sem_r.at[n],
            device_id=device, device_id_type=MESH,
        )
        copy.start()
        sent.append(copy)
        return copy

    def drain():
        for copy in sent:
            copy.wait_send()
        sent.clear()

    loads = [
        pltpu.make_async_copy(y_hbm, yf.at[core], in_sem.at[0]),
        pltpu.make_async_copy(x_hbm.at[0, :, core], xf.at[:, 0], in_sem.at[1]),
        pltpu.make_async_copy(x_hbm.at[1, :, core], xf.at[:, 1], in_sem.at[2]),
    ]
    for copy in loads:
        copy.start()

    barrier = pltpu.get_barrier_semaphore()
    peers = (
        [at(dz=d) for d in OTHERS_Z] + [at(dx=d) for d in OTHERS_4]
        + [at(dy=a, dc=c) for a, c in GROUP_YC]
    )
    for peer in peers:
        pl.semaphore_signal(barrier, inc=1, device_id=peer, device_id_type=MESH)

    lane = lax.broadcasted_iota(jnp.int32, (16, L), 1)
    first = core == 0

    def mine(ref):
        low, high = ref[0:16, :], ref[16:32, :]
        low_r, high_r = pltpu.roll(low, 64, 1), pltpu.roll(high, 64, 1)
        return jnp.where(lane < 64, jnp.where(first, low, low_r), jnp.where(first, high_r, high))

    def spread(vec, dst, start):
        for m in range(vec.shape[0]):
            here = start + m * L
            dst[here:here + L, :] = jnp.broadcast_to(vec[m:m + 1, :], (L, L)).T

    def gather_rows(src, chunk, dst):
        for m in range(8):
            here = chunk * HALF + m * L
            dst[m:m + 1, :] = jnp.sum(src[here:here + L, :].T, axis=0, keepdims=True)

    axd[...] = mine(ax_ref)
    spread(mine(sx_ref), ub, 0)
    syv[core] = sy_ref[...]
    ayv[core] = ay_ref[...]
    for copy in loads:
        copy.wait()

    def cast_x(i, _):
        xb[pl.ds(i * L, 64), :] = xf[i, 0].astype(BF16)
        xb[pl.ds(i * L + 64, 64), :] = xf[i, 1].astype(BF16)
        return 0
    lax.fori_loop(0, 16, cast_x, 0)

    def cast_y(half):
        def step(i, _):
            yb[half, pl.ds(i * L, L), :] = yf[half, pl.ds(i * L, L), :].astype(BF16)
            return 0
        lax.fori_loop(0, 8, step, 0)
    cast_y(core)

    def fold8(v):
        return jnp.sum(v.reshape(-1, 8, L), axis=0)

    def make_plan(half, i, fresh):
        rows = slice(i * HALF, (i + 1) * HALF)
        u = ub[rows, :]
        if fresh:
            acc_r = acc_m = None
        else:
            acc_r, acc_m = rt[rows, :], mx[rows, :]
        for j in range(4):
            s = lax.dot_general(
                xb[rows, :], yb[half, j * 256:(j + 1) * 256, :],
                (((1,), (1,)), ((), ())), preferred_element_type=F32,
            )
            for l in range(2):
                t = j * 2 + l
                p = (u * jnp.exp(s[:, l * L:(l + 1) * L] * FACTOR)) * syv[half, t:t + 1, :]
                plan[half, rows, t * L:(t + 1) * L] = p
                pa = p * ayv[half, t:t + 1, :]
                acc_r = p if acc_r is None else acc_r + p
                acc_m = pa if acc_m is None else acc_m + pa
                c = fold8(p)
                colacc[half, t] = c if i == 0 else colacc[half, t] + c
        rt[rows, :] = acc_r
        mx[rows, :] = acc_m

    sib = at(dc=1)
    make_plan(core, 0, True)
    pl.semaphore_wait(barrier, len(peers))
    fetch = [
        send(y_hbm, yf.at[core], sib),
        send(sy_ref, syv.at[core], sib),
        send(ay_ref, ayv.at[core], sib),
    ]
    make_plan(core, 1, True)
    for copy in fetch:
        copy.wait_recv()
    cast_y(other)

    def rows_x(k, n, c):
        return [
            send(vrow.at[k, c, 0:n], xrow.at[k, c, q, 0:n], at(dx=d))
            for q, d in enumerate(OTHERS_4)
        ]

    def rows_z(k, n, c, copies):
        for copy in copies:
            copy.wait_recv()
        total = vrow[k, c, 0:n]
        for q in range(3):
            total = total + xrow[k, c, q, 0:n]
        zsrc[k, c, 0:n] = total
        return [
            send(zsrc.at[k, c, 0:n], zrow.at[k, c, q, 0:n], at(dz=d))
            for q, d in enumerate(OTHERS_Z)
        ]

    def rows_end(k, n, c, copies):
        for copy in copies:
            copy.wait_recv()
        total = zsrc[k, c, 0:n]
        for q in range(7):
            total = total + zrow[k, c, q, 0:n]
        return total

    in_x = []
    for c in range(2):
        make_plan(other, c, False)
        gather_rows(rt, c, vrow.at[0, c, 0])
        gather_rows(mx, c, vrow.at[0, c, 1])
        in_x.append(rows_x(0, 2, c))
    in_z = [rows_z(0, 2, c, in_x[c]) for c in range(2)]
    for half in range(2):
        for t in range(8):
            vcol[0, half * 8 + t:half * 8 + t + 1, :] = jnp.sum(
                colacc[half, t], axis=0, keepdims=True)

    def turn_x(i, _):
        rows = pl.ds(pl.multiple_of(i * L, L), L)
        xt[:, rows] = xb[rows, :].T
        return 0
    lax.fori_loop(0, 16, turn_x, 0)

    def back(c):
        for half in range(2):
            def strip(i, cols):
                rows = pl.ds(pl.multiple_of(c * HALF + i * STRIP, STRIP), STRIP)
                r = rowb[rows, :]
                return tuple(
                    cols[t] + fold8(plan[half, rows, t * L:(t + 1) * L] * r) for t in range(8)
                )
            init = tuple(jnp.zeros((8, L), F32) if c == 0 else colacc[half, t] for t in range(8))
            cols = lax.fori_loop(0, HALF // STRIP, strip, init)
            for t in range(8):
                colacc[half, t] = cols[t]

    def back_end(dst):
        for half in range(2):
            for t in range(8):
                dst[half * 8 + t:half * 8 + t + 1, :] = jnp.sum(
                    colacc[half, t], axis=0, keepdims=True)

    def sum_cols(src, dst):
        copies = [
            send(src, dst.at[q], at(dy=a, dc=c)) for q, (a, c) in enumerate(GROUP_YC)
        ]
        for copy in copies:
            copy.wait_recv()
        total = src[...]
        for q in range(7):
            total = total + dst[q]
        return total

    for c in range(2):
        total = rows_end(0, 2, c, in_z[c])
        rtot[c * 8:(c + 1) * 8, :] = total[0]
        spread(axd[c * 8:(c + 1) * 8, :] - total[1] / total[0], rowb, c * HALF)
        back(c)
    back_end(vcol.at[1])
    total = sum_cols(vcol, crow)
    ay_all = ayv[...].reshape(16, L)
    ctot[...] = total[0]
    avec[...] = ay_all - total[1] / total[0]

    in_x = []
    for c in range(2):
        def mix(i, _):
            rows = pl.ds(pl.multiple_of(c * HALF + i * STRIP, STRIP), STRIP)
            acc = jnp.zeros((STRIP, L), F32)
            for half in range(2):
                for t in range(8):
                    acc += plan[half, rows, t * L:(t + 1) * L] * avec[half * 8 + t:half * 8 + t + 1, :]
            mx[rows, :] = acc
            return 0
        lax.fori_loop(0, HALF // STRIP, mix, 0)
        gather_rows(mx, c, vrow.at[1, c, 0])
        in_x.append(rows_x(1, 1, c))
    in_z = [rows_z(1, 1, c, in_x[c]) for c in range(2)]
    for c in range(2):
        total = rows_end(1, 1, c, in_z[c])
        spread(axd[c * 8:(c + 1) * 8, :] - total[0] / rtot[c * 8:(c + 1) * 8, :], rowb, c * HALF)
        back(c)
    back_end(vcol2)
    avec[...] = ay_all - sum_cols(vcol2, crow2) / ctot[...]

    par = lax.rem(x, 2)

    def weigh(order):
        side = par if order == 0 else 1 - par
        rows = pl.ds(pl.multiple_of(side * HALF, HALF), HALF)
        r = rowb[rows, :]
        for half in range(2):
            for t in range(8):
                a = avec[half * 8 + t:half * 8 + t + 1, :]
                w = plan[half, rows, t * L:(t + 1) * L] * (r + a)
                wts[half, rows, t * L:(t + 1) * L] = w.astype(BF16)
        g = jnp.dot(wts[0, rows, :], yb[0], preferred_element_type=F32)
        g += jnp.dot(wts[1, rows, :], yb[1], preferred_element_type=F32)
        g = g * FACTOR
        for m in range(8):
            off = lax.rem(m + 8 - z, 8)
            pos = lax.rem(off + 6, 8)
            for h in range(2):
                xo = lax.rem(2 * h + side + 4 - x, 4)
                piece = g[m * L + h * 64:m * L + h * 64 + 64, :]
                ga[xo, pos] = piece[0:RA, :]
                gb[off, order, xo // 2] = piece[RA:64, :]

    right_x, left_x = at(dx=1), at(dx=3)
    right_z, left_z = at(dz=1), at(dz=7)
    right_y, left_y = at(dy=1), at(dy=3)

    def lo(c):
        return slice(4 * c, 4 * c + 2)

    def hi(c):
        return slice(4 * c + 2, 4 * c + 4)

    weigh(0)
    one_a = [None, None]
    two_a = [[], []]
    for c in range(2):
        one_a[c] = (
            send(ga.at[2, lo(c)], a1.at[c, 0], right_x), send(ga.at[2, hi(c)], a1.at[c, 1], left_x)
        )
    one_b = [send(gb.at[4, 0], b1.at[0], right_z), None]
    fwd = [[None, None], [None, None], [None, None]]
    bwd = [[None, None], [None, None], [None, None]]
    bwd[0][0] = send(gb.at[5, 0], bm.at[0, 0], left_z)
    weigh(1)

    def a_direct(c):
        two_a[c].append(send(ga.at[1, hi(c)], a2.at[0, hi(c)], right_x))
        two_a[c].append(send(ga.at[3, lo(c)], a2.at[1, lo(c)], left_x))

    def a_summed(c):
        one_a[c][0].wait_recv()
        ga[1, lo(c)] = ga[1, lo(c)] + a1[c, 0]
        two_a[c].append(send(ga.at[1, lo(c)], a2.at[0, lo(c)], right_x))
        one_a[c][1].wait_recv()
        ga[3, hi(c)] = ga[3, hi(c)] + a1[c, 1]
        two_a[c].append(send(ga.at[3, hi(c)], a2.at[1, hi(c)], left_x))

    last_a = []

    def a_end(c):
        for copy in two_a[c]:
            copy.wait_recv()
        here = slice(4 * c, 4 * c + 4)
        ga[0, here] = ga[0, here] + a2[0, here] + a2[1, here]
        for p in FAR_Z if c == 0 else NEAR_Z:
            last_a.append(send(ga.at[0, p], az.at[len(last_a)], at(dz=(p + 2) % 8)))

    a_direct(0)
    one_b[1] = send(gb.at[4, 1], b1.at[1], left_z)
    fwd[0][1] = send(gb.at[3, 1], bp.at[0, 1], right_z)

    def cols_of(half, part, dst):
        g = jnp.dot(xt[...], wts[half, :, part * 512:(part + 1) * 512], preferred_element_type=F32)
        g = g * FACTOR
        for q in range(4):
            off = lax.rem(q + 4 - row, 4)
            for h in range(2):
                dst[part, off, h] = g[q * 64 + h * 32:q * 64 + h * 32 + 32, :]

    swap = []
    for part in range(2):
        cols_of(other, part, gyo)
        swap.append(send(gyo.at[part], gyc.at[part], sib))

    a_summed(0)
    a_direct(1)
    one_b[0].wait_recv()
    gb[3, 0] = gb[3, 0] + b1[0]
    fwd[0][0] = send(gb.at[3, 0], bp.at[0, 0], right_z)
    one_b[1].wait_recv()
    gb[5, 1] = gb[5, 1] + b1[1]
    bwd[0][1] = send(gb.at[5, 1], bm.at[0, 1], left_z)
    a_summed(1)

    one_y = [None, None]
    two_y = [[], []]

    def y_start(part):
        cols_of(core, part, gy)
        swap[part].wait_recv()
        gy[part] = gy[part] + gyc[part]
        one_y[part] = (
            send(gy.at[part, 2, 0], y1.at[part, 0], right_y),
            send(gy.at[part, 2, 1], y1.at[part, 1], left_y),
        )

    def y_direct(part):
        two_y[part].append(send(gy.at[part, 1, 1], y2.at[0, part, 1], right_y))
        two_y[part].append(send(gy.at[part, 3, 0], y2.at[1, part, 0], left_y))

    def y_summed(part):
        one_y[part][0].wait_recv()
        gy[part, 1, 0] = gy[part, 1, 0] + y1[part, 0]
        two_y[part].append(send(gy.at[part, 1, 0], y2.at[0, part, 0], right_y))
        one_y[part][1].wait_recv()
        gy[part, 3, 1] = gy[part, 3, 1] + y1[part, 1]
        two_y[part].append(send(gy.at[part, 3, 1], y2.at[1, part, 1], left_y))

    def y_end(part):
        for copy in two_y[part]:
            copy.wait_recv()
        for h in range(2):
            gy_ref[h * 32:(h + 1) * 32, part * 512:(part + 1) * 512] = (
                gy[part, 0, h] + y2[0, part, h] + y2[1, part, h]
            )

    def z_fwd(s, p):
        fwd[s - 3][p].wait_recv()
        gb[5 - s, p] = gb[5 - s, p] + bp[s - 3, p]
        fwd[s - 2][p] = send(gb.at[5 - s, p], bp.at[s - 2, p], right_z)

    def z_bwd(s, p):
        bwd[s - 3][p].wait_recv()
        gb[3 + s, p] = gb[3 + s, p] + bm[s - 3, p]
        bwd[s - 2][p] = send(gb.at[3 + s, p], bm.at[s - 2, p], left_z)

    last_b = []

    def b_end(p):
        fwd[2][p].wait_recv()
        bwd[2][p].wait_recv()
        gb[0, p] = gb[0, p] + bp[2, p] + bm[2, p]
        for h in range(2):
            if (h, p) != (0, 0):
                last_b.append(send(gb.at[0, p, h], bx.at[len(last_b)], at(dx=2 * h + p)))

    y_start(0)
    z_bwd(3, 0)
    z_fwd(3, 1)
    y_start(1)
    y_direct(0)
    z_fwd(3, 0)
    z_bwd(3, 1)
    y_direct(1)
    a_end(0)
    z_bwd(4, 0)
    z_fwd(4, 1)
    y_summed(0)
    a_end(1)
    z_fwd(4, 0)
    z_bwd(4, 1)
    y_summed(1)
    b_end(1)
    b_end(0)
    y_end(0)
    y_end(1)
    total = ga[0, 6]
    for q in range(7):
        last_a[q].wait_recv()
        total = total + az[q]
    gx_ref[0:RA, :] = total
    total = gb[0, 0, 0]
    for q in range(3):
        last_b[q].wait_recv()
        total = total + bx[q]
    gx_ref[RA:64, :] = total
    drain()


def finish(a_ref, b_ref, gx_ref, gy_ref):
    gx_ref[...] = a_ref[...]
    gy_ref[...] = b_ref[...]


def body(features_x, scale_x, adjoint_x, features_y, scale_y, adjoint_y):
    vmem = pl.BlockSpec(memory_space=pltpu.VMEM)
    anym = pl.BlockSpec(memory_space=pl.ANY)
    V = pltpu.VMEM
    ncopies = 107
    shapes = (
        jax.ShapeDtypeStruct((64, WIDTH), F32),
        jax.ShapeDtypeStruct((64, 1024), F32),
    )
    parts = pl.pallas_call(
        kernel,
        out_shape=shapes,
        in_specs=[vmem, vmem, vmem, vmem, anym, anym],
        out_specs=(vmem, vmem),
        scratch_shapes=[
            V((16, 2, 64, WIDTH), F32), V((2, 1024, WIDTH), F32),
            V((2048, WIDTH), BF16), V((2, 1024, WIDTH), BF16), V((WIDTH, 2048), BF16),
            V((2, 2048, 1024), F32), V((2, 2048, 1024), BF16),
            V((2, 8, L), F32), V((2, 8, L), F32),
            V((2048, L), F32), V((2048, L), F32), V((2048, L), F32), V((2048, L), F32),
            V((16, L), F32), V((2, 8, 8, L), F32),
            V((2, 2, 2, 8, L), F32), V((2, 2, 3, 2, 8, L), F32),
            V((2, 2, 2, 8, L), F32), V((2, 2, 7, 2, 8, L), F32),
            V((2, 16, L), F32), V((7, 2, 16, L), F32),
            V((16, L), F32), V((7, 16, L), F32), V((16, L), F32), V((16, L), F32), V((16, L), F32),
            V((4, 8, RA, WIDTH), F32), V((8, 2, 2, RB, WIDTH), F32),
            V((2, 2, 2, RA, WIDTH), F32), V((2, 8, RA, WIDTH), F32), V((7, RA, WIDTH), F32),
            V((2, 2, RB, WIDTH), F32), V((3, 2, 2, RB, WIDTH), F32), V((3, 2, 2, RB, WIDTH), F32),
            V((3, RB, WIDTH), F32),
            V((2, 4, 2, 32, 512), F32), V((2, 4, 2, 32, 512), F32), V((2, 4, 2, 32, 512), F32),
            V((2, 2, 32, 512), F32), V((2, 2, 2, 32, 512), F32),
            pltpu.SemaphoreType.DMA((3,)),
            pltpu.SemaphoreType.DMA((ncopies,)), pltpu.SemaphoreType.DMA((ncopies,)),
        ],
        compiler_params=pltpu.CompilerParams(
            collective_id=0, has_side_effects=True, vmem_limit_bytes=56 * 2**20
        ),
        cost_estimate=pl.CostEstimate(
            flops=6 * 2048 * 2048 * 256, bytes_accessed=5 * 2**20, transcendentals=2048 * 2048
        ),
        name="sinkhorn_adjoint",
    )(
        scale_x.reshape(32, L), adjoint_x.reshape(32, L),
        scale_y.reshape(8, L), adjoint_y.reshape(8, L),
        features_x.reshape(2, 16, 2, 64, WIDTH), features_y,
    )
    gx, gy = pl.pallas_call(
        finish, out_shape=shapes, in_specs=[vmem, vmem], out_specs=(vmem, vmem), name="finish",
    )(*parts)
    return gx, gy.T


def solution(mesh):
    in_specs = (P("row", None), P("row"), P("row"), P("col", None), P("col"), P("col"))
    out_specs = (P(("row", "col"), None), P("col", "row"))
    return jax.shard_map(body, mesh=mesh, in_specs=in_specs, out_specs=out_specs, check_vma=False)
```

time: 782 us -> 75.5 us (0.10)
  blocking collectives: 513 us -> 0 us
  waiting for transfers between devices: 164 us -> 0 us
  Pallas kernels: 0 us -> 73.6 us
  matrix products: 72.8 us -> 0 us
  between operations: 14.1 us -> 0.64 us
  local copies, waits for them, and re-layouts: 8.93 us -> 0 us
    psum x4 -> x0, blocking collectives: 513 us -> none  [the longest x2 495 us: finish_rows(): return base - lax.psum(partial_value, 'col') / totals]
    reduce_scatter x2 -> x0, waiting for transfers between devices: 164 us -> none  [the longest x1 148 us: body(): grad_x = lax.psum_scatter(row_stack, 'col', scatter_dimension=0, tiled=True)]
    pallas_call x0 -> x2, Pallas kernels: none -> 73.6 us  [the longest x1 71.8 us: body(): pl.pallas_call(kernel, out_shape=shapes, in_specs=[vmem, vmem, vmem, vmem...]
    dot_general x7 -> x0, matrix products: 72.8 us -> none  [the longest x2 31.8 us: mix_fn(): return (acc, jnp.dot(fetch(), current, precision=lax.Precision.HIGHEST))]
    unnamed x12 -> x0, local copies, waits for them, and re-layouts: 8.93 us -> none
  transfers between devices with their start and end apart: 2 -> 0, of which waited for: 2 -> 0; matrix products, arithmetic and copies ran while one was open for 1% -> 0% of each run, Pallas kernels for 0% -> 0%
where the time goes in v2:
time: 75.5 us; the launch traced here: 74.2 us
  Pallas kernels  73.6 us (97%)
    pallas_call x1, Pallas kernels, body(): pl.pallas_call(kernel, out_shape=shapes, in_specs=[vmem, vmem, vmem, vmem...  71.8 us
    pallas_call x1, Pallas kernels, body(): pl.pallas_call(finish, out_shape=shapes, in_specs=[vmem, vmem], out_specs...  1.72 us

profile of v2, /device:TPU:32, one launch (start us, length us, event | category | flops | bytes accessed | tf_op | source)
XLA Modules:
  0.0 74.2 jit_solution(3164803051303284119)
XLA Ops:
  0.6 71.8 %sinkhorn_adjoint.1 = (f32[64,256]{1,0:T(8,128)}, f32[64,1024]{1,0:T(8,128)}) custom-call(f32[32,128]{1,0:T(8,128)} %bitcast.8, f32[32,128]{1,0:T(8,128)} %bitcast.9, f32[8,128]{1,0:T(8,128)} %bitcast.10, f32[8,128]{1,0:T(8,128)} %bitcast.11, f32[2,16,2,64,256]{4,3,2,1,0:T(8,128)} %bitcast.6, f32[1024,256]{1,0:T(8,128)} %y_hbm.1), custom_call_target="tpu_custom_call" | custom-call | flops 6442450944 | bytes 5242880 | tf_op jit(solution)/shard_map/sinkhorn_adjoint/pallas_call | solution.py:463
  72.5 1.7 %finish.1 = (f32[64,256]{1,0:T(8,128)}, f32[64,1024]{1,0:T(8,128)}) custom-call(f32[64,256]{1,0:T(8,128)} %get-tuple-element.6.a_ref, f32[64,1024]{1,0:T(8,128)} %get-tuple-element.7.b_ref), custom_call_target="tpu_custom_call" | custom-call | tf_op jit(solution)/shard_map/finish/pallas_call | solution.py:500

commit v3 on v2

--- a/solution.py
+++ b/solution.py
@@ -22,8 +22,7 @@
 RB = 64 - RA
 OTHERS_Z = (4, 3, 5, 2, 6, 1, 7)
 OTHERS_4 = (2, 1, 3)
-FAR_Z = (2, 1, 3, 0)
-NEAR_Z = (4, 5, 7)
+RC = 24
 GROUP_YC = tuple((a, c) for a in (2, 1, 3, 0) for c in (0, 1) if (a, c) != (0, 0))
 
 
@@ -123,8 +122,8 @@
     def fold8(v):
         return jnp.sum(v.reshape(-1, 8, L), axis=0)
 
-    def make_plan(half, i, fresh):
-        rows = slice(i * HALF, (i + 1) * HALF)
+    def make_plan(half, start, size, fresh):
+        rows = slice(start, start + size)
         u = ub[rows, :]
         if fresh:
             acc_r = acc_m = None
@@ -143,19 +142,19 @@
                 acc_r = p if acc_r is None else acc_r + p
                 acc_m = pa if acc_m is None else acc_m + pa
                 c = fold8(p)
-                colacc[half, t] = c if i == 0 else colacc[half, t] + c
+                colacc[half, t] = c if start == 0 else colacc[half, t] + c
         rt[rows, :] = acc_r
         mx[rows, :] = acc_m
 
     sib = at(dc=1)
-    make_plan(core, 0, True)
+    make_plan(core, 0, 512, True)
     pl.semaphore_wait(barrier, len(peers))
     fetch = [
         send(y_hbm, yf.at[core], sib),
         send(sy_ref, syv.at[core], sib),
         send(ay_ref, ayv.at[core], sib),
     ]
-    make_plan(core, 1, True)
+    make_plan(core, 512, 1536, True)
     for copy in fetch:
         copy.wait_recv()
     cast_y(other)
@@ -188,7 +187,7 @@
 
     in_x = []
     for c in range(2):
-        make_plan(other, c, False)
+        make_plan(other, c * HALF, HALF, False)
         gather_rows(rt, c, vrow.at[0, c, 0])
         gather_rows(mx, c, vrow.at[0, c, 1])
         in_x.append(rows_x(0, 2, c))
@@ -324,6 +323,8 @@
         ga[3, hi(c)] = ga[3, hi(c)] + a1[c, 1]
         two_a[c].append(send(ga.at[3, hi(c)], a2.at[1, hi(c)], left_x))
 
+    up2, down2 = at(dz=2), at(dz=6)
+    relay = []
     last_a = []
 
     def a_end(c):
@@ -331,8 +332,26 @@
             copy.wait_recv()
         here = slice(4 * c, 4 * c + 4)
         ga[0, here] = ga[0, here] + a2[0, here] + a2[1, here]
-        for p in FAR_Z if c == 0 else NEAR_Z:
-            last_a.append(send(ga.at[0, p], az.at[len(last_a)], at(dz=(p + 2) % 8)))
+        if c == 0:
+            relay.append(send(ga.at[0, 2, 0:RC], az.at[0, 0:RC], up2))
+            relay.append(send(ga.at[0, 2, RC:RA], az.at[0, RC:RA], down2))
+            relay.append(send(ga.at[0, 1], az.at[1], right_z))
+            relay.append(send(ga.at[0, 3], az.at[2], left_z))
+        else:
+            last_a.append(send(ga.at[0, 7], az.at[3], right_z))
+            last_a.append(send(ga.at[0, 5], az.at[4], left_z))
+
+    def a_relay():
+        relay[0].wait_recv()
+        relay[2].wait_recv()
+        ga[0, 0, 0:RC] = ga[0, 0, 0:RC] + az[0, 0:RC] + az[1, 0:RC]
+        ga[0, 0, RC:RA] = ga[0, 0, RC:RA] + az[1, RC:RA]
+        last_a.append(send(ga.at[0, 0], az.at[5], up2))
+        relay[1].wait_recv()
+        relay[3].wait_recv()
+        ga[0, 4, 0:RC] = ga[0, 4, 0:RC] + az[2, 0:RC]
+        ga[0, 4, RC:RA] = ga[0, 4, RC:RA] + az[0, RC:RA] + az[2, RC:RA]
+        last_a.append(send(ga.at[0, 4], az.at[6], down2))
 
     a_direct(0)
     one_b[1] = send(gb.at[4, 1], b1.at[1], left_z)
@@ -350,16 +369,6 @@
     for part in range(2):
         cols_of(other, part, gyo)
         swap.append(send(gyo.at[part], gyc.at[part], sib))
-
-    a_summed(0)
-    a_direct(1)
-    one_b[0].wait_recv()
-    gb[3, 0] = gb[3, 0] + b1[0]
-    fwd[0][0] = send(gb.at[3, 0], bp.at[0, 0], right_z)
-    one_b[1].wait_recv()
-    gb[5, 1] = gb[5, 1] + b1[1]
-    bwd[0][1] = send(gb.at[5, 1], bm.at[0, 1], left_z)
-    a_summed(1)
 
     one_y = [None, None]
     two_y = [[], []]
@@ -413,36 +422,47 @@
             if (h, p) != (0, 0):
                 last_b.append(send(gb.at[0, p, h], bx.at[len(last_b)], at(dx=2 * h + p)))
 
+    one_b[0].wait_recv()
+    gb[3, 0] = gb[3, 0] + b1[0]
+    fwd[0][0] = send(gb.at[3, 0], bp.at[0, 0], right_z)
+    z_bwd(3, 0)
+    a_summed(0)
+    a_direct(1)
+    z_fwd(3, 1)
+    one_b[1].wait_recv()
+    gb[5, 1] = gb[5, 1] + b1[1]
+    bwd[0][1] = send(gb.at[5, 1], bm.at[0, 1], left_z)
+    a_summed(1)
     y_start(0)
-    z_bwd(3, 0)
-    z_fwd(3, 1)
+    z_fwd(3, 0)
+    z_bwd(4, 0)
     y_start(1)
     y_direct(0)
-    z_fwd(3, 0)
+    y_direct(1)
+    z_fwd(4, 1)
     z_bwd(3, 1)
-    y_direct(1)
     a_end(0)
-    z_bwd(4, 0)
-    z_fwd(4, 1)
+    z_fwd(4, 0)
     y_summed(0)
+    z_bwd(4, 1)
     a_end(1)
-    z_fwd(4, 0)
-    z_bwd(4, 1)
     y_summed(1)
+    a_relay()
+    b_end(0)
     b_end(1)
-    b_end(0)
     y_end(0)
     y_end(1)
     total = ga[0, 6]
-    for q in range(7):
+    for q in range(4):
         last_a[q].wait_recv()
-        total = total + az[q]
+        total = total + az[3 + q]
     gx_ref[0:RA, :] = total
     total = gb[0, 0, 0]
     for q in range(3):
         last_b[q].wait_recv()
         total = total + bx[q]
     gx_ref[RA:64, :] = total
+    assert count[0] == sem_s.shape[0]
     drain()
 
 
@@ -455,7 +475,7 @@
     vmem = pl.BlockSpec(memory_space=pltpu.VMEM)
     anym = pl.BlockSpec(memory_space=pl.ANY)
     V = pltpu.VMEM
-    ncopies = 107
+    ncopies = 108
     shapes = (
         jax.ShapeDtypeStruct((64, WIDTH), F32),
         jax.ShapeDtypeStruct((64, 1024), F32),

time: 75.5 us -> 69.6 us (0.922); the launches traced: 74.2 us -> 69.4 us
  Pallas kernels: 73.6 us -> 68.8 us
    pallas_call x1, Pallas kernels: 71.8 us -> 67.1 us  [body(): pl.pallas_call(kernel, out_shape=shapes, in_specs=[vmem, vmem, vmem, vmem...]
where the time goes in v3:
time: 69.6 us; the launch traced here: 69.4 us
  Pallas kernels  68.8 us (99%)
    pallas_call x1, Pallas kernels, body(): pl.pallas_call(kernel, out_shape=shapes, in_specs=[vmem, vmem, vmem, vmem...  67.1 us
    pallas_call x1, Pallas kernels, body(): pl.pallas_call(finish, out_shape=shapes, in_specs=[vmem, vmem], out_specs...  1.72 us

profile of v3, /device:TPU:32, one launch (start us, length us, event | category | flops | bytes accessed | tf_op | source)
XLA Modules:
  0.0 69.4 jit_solution(1800133068627401948)
XLA Ops:
  0.6 67.1 %sinkhorn_adjoint.1 = (f32[64,256]{1,0:T(8,128)}, f32[64,1024]{1,0:T(8,128)}) custom-call(f32[32,128]{1,0:T(8,128)} %bitcast.8, f32[32,128]{1,0:T(8,128)} %bitcast.9, f32[8,128]{1,0:T(8,128)} %bitcast.10, f32[8,128]{1,0:T(8,128)} %bitcast.11, f32[2,16,2,64,256]{4,3,2,1,0:T(8,128)} %bitcast.6, f32[1024,256]{1,0:T(8,128)} %y_hbm.1), custom_call_target="tpu_custom_call" | custom-call | flops 6442450944 | bytes 5242880 | tf_op jit(solution)/shard_map/sinkhorn_adjoint/pallas_call | solution.py:483
  67.7 1.7 %finish.1 = (f32[64,256]{1,0:T(8,128)}, f32[64,1024]{1,0:T(8,128)}) custom-call(f32[64,256]{1,0:T(8,128)} %get-tuple-element.6.a_ref, f32[64,1024]{1,0:T(8,128)} %get-tuple-element.7.b_ref), custom_call_target="tpu_custom_call" | custom-call | tf_op jit(solution)/shard_map/finish/pallas_call | solution.py:520

commit v4 on v3

--- a/solution.py
+++ b/solution.py
@@ -11,6 +11,7 @@
 KERNEL_GAIN = 0.5
 WIDTH = 256
 FACTOR = KERNEL_GAIN / math.sqrt(WIDTH)
+FACTOR2 = FACTOR / math.log(2.0)
 L = 128
 F32 = jnp.float32
 BF16 = jnp.bfloat16
@@ -29,7 +30,7 @@
 def kernel(
     sx_ref, ax_ref, sy_ref, ay_ref, x_hbm, y_hbm, gx_ref, gy_ref,
     xf, yf, xb, yb, xt, plan, wts, syv, ayv, rowb, ub, rt, mx, axd, colacc,
-    vrow, xrow, zsrc, zrow, vcol, crow, vcol2, crow2, avec, rtot, ctot,
+    vrow, xrow, zsrc, zrow, vcol, crow, avec, rtot, ctot,
     ga, gb, a1, a2, az, b1, bp, bm, bx, gy, gyo, gyc, y1, y2,
     in_sem, sem_s, sem_r,
 ):
@@ -67,8 +68,10 @@
 
     loads = [
         pltpu.make_async_copy(y_hbm, yf.at[core], in_sem.at[0]),
-        pltpu.make_async_copy(x_hbm.at[0, :, core], xf.at[:, 0], in_sem.at[1]),
-        pltpu.make_async_copy(x_hbm.at[1, :, core], xf.at[:, 1], in_sem.at[2]),
+        pltpu.make_async_copy(x_hbm.at[0, 0:4, core], xf.at[0:4, 0], in_sem.at[1]),
+        pltpu.make_async_copy(x_hbm.at[1, 0:4, core], xf.at[0:4, 1], in_sem.at[2]),
+        pltpu.make_async_copy(x_hbm.at[0, 4:16, core], xf.at[4:16, 0], in_sem.at[3]),
+        pltpu.make_async_copy(x_hbm.at[1, 4:16, core], xf.at[4:16, 1], in_sem.at[4]),
     ]
     for copy in loads:
         copy.start()
@@ -100,17 +103,17 @@
             dst[m:m + 1, :] = jnp.sum(src[here:here + L, :].T, axis=0, keepdims=True)
 
     axd[...] = mine(ax_ref)
-    spread(mine(sx_ref), ub, 0)
+    spread(jnp.log2(mine(sx_ref)), ub, 0)
     syv[core] = sy_ref[...]
     ayv[core] = ay_ref[...]
-    for copy in loads:
+    for copy in loads[0:3]:
         copy.wait()
 
     def cast_x(i, _):
         xb[pl.ds(i * L, 64), :] = xf[i, 0].astype(BF16)
         xb[pl.ds(i * L + 64, 64), :] = xf[i, 1].astype(BF16)
         return 0
-    lax.fori_loop(0, 16, cast_x, 0)
+    lax.fori_loop(0, 4, cast_x, 0)
 
     def cast_y(half):
         def step(i, _):
@@ -136,7 +139,7 @@
             )
             for l in range(2):
                 t = j * 2 + l
-                p = (u * jnp.exp(s[:, l * L:(l + 1) * L] * FACTOR)) * syv[half, t:t + 1, :]
+                p = jnp.exp2(s[:, l * L:(l + 1) * L] * FACTOR2 + u) * syv[half, t:t + 1, :]
                 plan[half, rows, t * L:(t + 1) * L] = p
                 pa = p * ayv[half, t:t + 1, :]
                 acc_r = p if acc_r is None else acc_r + p
@@ -154,6 +157,9 @@
         send(sy_ref, syv.at[core], sib),
         send(ay_ref, ayv.at[core], sib),
     ]
+    for copy in loads[3:]:
+        copy.wait()
+    lax.fori_loop(4, 16, cast_x, 0)
     make_plan(core, 512, 1536, True)
     for copy in fetch:
         copy.wait_recv()
@@ -191,11 +197,28 @@
         gather_rows(rt, c, vrow.at[0, c, 0])
         gather_rows(mx, c, vrow.at[0, c, 1])
         in_x.append(rows_x(0, 2, c))
+    def back_end(dst):
+        for half in range(2):
+            for t in range(8):
+                dst[half * 8 + t:half * 8 + t + 1, :] = jnp.sum(
+                    colacc[half, t], axis=0, keepdims=True)
+
+    def cols_start(k):
+        return [
+            send(vcol.at[k], crow.at[k, q], at(dy=a, dc=c)) for q, (a, c) in enumerate(GROUP_YC)
+        ]
+
+    def cols_end(k, copies):
+        for copy in copies:
+            copy.wait_recv()
+        total = vcol[k]
+        for q in range(7):
+            total = total + crow[k, q]
+        return total
+
     in_z = [rows_z(0, 2, c, in_x[c]) for c in range(2)]
-    for half in range(2):
-        for t in range(8):
-            vcol[0, half * 8 + t:half * 8 + t + 1, :] = jnp.sum(
-                colacc[half, t], axis=0, keepdims=True)
+    back_end(vcol.at[0])
+    in_col = cols_start(0)
 
     def turn_x(i, _):
         rows = pl.ds(pl.multiple_of(i * L, L), L)
@@ -216,33 +239,17 @@
             for t in range(8):
                 colacc[half, t] = cols[t]
 
-    def back_end(dst):
-        for half in range(2):
-            for t in range(8):
-                dst[half * 8 + t:half * 8 + t + 1, :] = jnp.sum(
-                    colacc[half, t], axis=0, keepdims=True)
-
-    def sum_cols(src, dst):
-        copies = [
-            send(src, dst.at[q], at(dy=a, dc=c)) for q, (a, c) in enumerate(GROUP_YC)
-        ]
-        for copy in copies:
-            copy.wait_recv()
-        total = src[...]
-        for q in range(7):
-            total = total + dst[q]
-        return total
-
     for c in range(2):
         total = rows_end(0, 2, c, in_z[c])
         rtot[c * 8:(c + 1) * 8, :] = total[0]
         spread(axd[c * 8:(c + 1) * 8, :] - total[1] / total[0], rowb, c * HALF)
         back(c)
     back_end(vcol.at[1])
-    total = sum_cols(vcol, crow)
+    more = cols_start(1)
     ay_all = ayv[...].reshape(16, L)
-    ctot[...] = total[0]
-    avec[...] = ay_all - total[1] / total[0]
+    col_tot = cols_end(0, in_col)
+    ctot[...] = col_tot
+    avec[...] = ay_all - cols_end(1, more) / col_tot
 
     in_x = []
     for c in range(2):
@@ -262,8 +269,8 @@
         total = rows_end(1, 1, c, in_z[c])
         spread(axd[c * 8:(c + 1) * 8, :] - total[0] / rtot[c * 8:(c + 1) * 8, :], rowb, c * HALF)
         back(c)
-    back_end(vcol2)
-    avec[...] = ay_all - sum_cols(vcol2, crow2) / ctot[...]
+    back_end(vcol.at[2])
+    avec[...] = ay_all - cols_end(2, cols_start(2)) / ctot[...]
 
     par = lax.rem(x, 2)
 
@@ -466,23 +473,14 @@
     drain()
 
 
-def finish(a_ref, b_ref, gx_ref, gy_ref):
-    gx_ref[...] = a_ref[...]
-    gy_ref[...] = b_ref[...]
-
-
 def body(features_x, scale_x, adjoint_x, features_y, scale_y, adjoint_y):
     vmem = pl.BlockSpec(memory_space=pltpu.VMEM)
     anym = pl.BlockSpec(memory_space=pl.ANY)
     V = pltpu.VMEM
-    ncopies = 108
-    shapes = (
-        jax.ShapeDtypeStruct((64, WIDTH), F32),
-        jax.ShapeDtypeStruct((64, 1024), F32),
-    )
-    parts = pl.pallas_call(
+    ncopies = 115
+    gx, gy = pl.pallas_call(
         kernel,
-        out_shape=shapes,
+        out_shape=(V((64, WIDTH), F32), V((64, 1024), F32)),
         in_specs=[vmem, vmem, vmem, vmem, anym, anym],
         out_specs=(vmem, vmem),
         scratch_shapes=[
@@ -494,15 +492,15 @@
             V((16, L), F32), V((2, 8, 8, L), F32),
             V((2, 2, 2, 8, L), F32), V((2, 2, 3, 2, 8, L), F32),
             V((2, 2, 2, 8, L), F32), V((2, 2, 7, 2, 8, L), F32),
-            V((2, 16, L), F32), V((7, 2, 16, L), F32),
-            V((16, L), F32), V((7, 16, L), F32), V((16, L), F32), V((16, L), F32), V((16, L), F32),
+            V((3, 16, L), F32), V((3, 7, 16, L), F32),
+            V((16, L), F32), V((16, L), F32), V((16, L), F32),
             V((4, 8, RA, WIDTH), F32), V((8, 2, 2, RB, WIDTH), F32),
             V((2, 2, 2, RA, WIDTH), F32), V((2, 8, RA, WIDTH), F32), V((7, RA, WIDTH), F32),
             V((2, 2, RB, WIDTH), F32), V((3, 2, 2, RB, WIDTH), F32), V((3, 2, 2, RB, WIDTH), F32),
             V((3, RB, WIDTH), F32),
             V((2, 4, 2, 32, 512), F32), V((2, 4, 2, 32, 512), F32), V((2, 4, 2, 32, 512), F32),
             V((2, 2, 32, 512), F32), V((2, 2, 2, 32, 512), F32),
-            pltpu.SemaphoreType.DMA((3,)),
+            pltpu.SemaphoreType.DMA((5,)),
             pltpu.SemaphoreType.DMA((ncopies,)), pltpu.SemaphoreType.DMA((ncopies,)),
         ],
         compiler_params=pltpu.CompilerParams(
@@ -517,9 +515,6 @@
         scale_y.reshape(8, L), adjoint_y.reshape(8, L),
         features_x.reshape(2, 16, 2, 64, WIDTH), features_y,
     )
-    gx, gy = pl.pallas_call(
-        finish, out_shape=shapes, in_specs=[vmem, vmem], out_specs=(vmem, vmem), name="finish",
-    )(*parts)
     return gx, gy.T
 
 

time: 69.6 us -> 67.9 us (0.976)
  Pallas kernels: 68.8 us -> 65.7 us
  local copies, waits for them, and re-layouts: 0 us -> 1.33 us
    pallas_call x2 -> x1, Pallas kernels: 68.8 us -> 65.7 us  [body(): pl.pallas_call(kernel, out_shape=(V((64, WIDTH), F32), V((64, 1024), F32)...]
    unnamed x0 -> x2, local copies, waits for them, and re-layouts: none -> 1.33 us
where the time goes in v4:
time: 67.9 us; the launch traced here: 67.7 us
  Pallas kernels  65.7 us (97%)
  local copies, waits for them, and re-layouts  1.33 us (2%)
    pallas_call x1, Pallas kernels, body(): pl.pallas_call(kernel, out_shape=(V((64, WIDTH), F32), V((64, 1024), F32)...  65.7 us

profile of v4, /device:TPU:32, one launch (start us, length us, event | category | flops | bytes accessed | tf_op | source)
XLA Modules:
  0.0 67.7 jit_solution(4987985227924656160)
XLA Ops:
  0.6 65.7 %sinkhorn_adjoint.1 = (f32[64,256]{1,0:T(8,128)S(1)}, f32[64,1024]{1,0:T(8,128)S(1)}) custom-call(f32[32,128]{1,0:T(8,128)} %bitcast.8, f32[32,128]{1,0:T(8,128)} %bitcast.9, f32[8,128]{1,0:T(8,128)} %bitcast.10, f32[8,128]{1,0:T(8,128)} %bitcast.11, f32[2,16,2,64,256]{4,3,2,1,0:T(8,128)} %bitcast.7, f32[1024,256]{1,0:T(8,128)} %y_hbm.1), custom_call_target="tpu_custom_call" | custom-call | flops 6442450944 | bytes 5242880 | tf_op jit(solution)/shard_map/sinkhorn_adjoint/pallas_call | solution.py:481
  66.4 0.6 copy.10
  67.0 0.7 %copy.11 = f32[1024,64]{0,1:T(8,128)} copy(f32[1024,64]{0,1:T(8,128)S(1)} %bitcast.6) | data formatting | bytes 524288
